TPU v7x, 512 devices: a whole 4x4x16 slice. The times are simulated.
512 devices in a mesh: seq: 64 (over x, z), head: 8 (over y, core).
Axes of the slice: x: 4, y: 4, z: 16, core: 2. Of those that a mesh axis runs over, the one named last changes fastest.
Arguments:
- tokens: bfloat16 [16384, 5376], P('seq', 'head'), may hold values from -6 to 6
- features: bfloat16 [512, 64, 1152], P('seq'), may hold values from -6 to 6
- starts: int32 [8], replicated, may hold values from 0 to 16128, as said below
- sources: int32 [8], replicated, may hold values from 0 to 56, as said below
- soft_gain: float32 [1152], replicated, may hold values from 0.25 to 1.75
- proj_weight: bfloat16 [1152, 5376], P(None, 'head'), may hold values from -0.1875 to 0.1875
- input_gain: float32 [5376], replicated, may hold values from 0.25 to 1.75
- query_weight: bfloat16 [5376, 2048], P('seq', 'head'), may hold values from -0.078125 to 0.078125
- key_weight: bfloat16 [5376, 1024], P('seq', 'head'), may hold values from -0.078125 to 0.078125
- value_weight: bfloat16 [5376, 1024], P('seq', 'head'), may hold values from -0.078125 to 0.078125
- query_gain: float32 [128], replicated, may hold values from 0.25 to 1.75
- key_gain: float32 [128], replicated, may hold values from 0.25 to 1.75
- out_weight: bfloat16 [2048, 5376], P('seq', 'head'), may hold values from -0.125 to 0.125
- post_gain: float32 [5376], P('head'), may hold values from 0.25 to 1.75
Outputs:
- layer_out: bfloat16 [16384, 5376], P('seq', 'head')
Inputs may be any that keep to these rules, and one draw needn't show every extreme that they name: Image i takes positions starts[i] to starts[i] + 255; the spans are in increasing order of i, do not intersect, and each crosses one boundary between sequence shards. Distinct multiples of 8; image i's patches fill feature rows sources[i] * 8 onward.
All inputs are finite; a program needn't handle non-finite values.
Results may differ from a plain program's by a relative error of at most 0.012.
Values may be sent and summed in bfloat16 or wider, within the bound.
No kernel may reach another device: no remote copies, remote signals or barrier semaphores. Data moves between devices by JAX's collectives and lax.ppermute only.
A program may use at most 64 MiB of HBM per device.

v0:
```python
import jax
import jax.numpy as jnp
from jax import lax
from jax.sharding import PartitionSpec as P

D = 5376
HEAD_DIM = 128
WINDOW = 1024
PATCH_SIDE = 64
POOL = 4
IMG_TOK = 256
EPSILON = 1e-06
QUERY_SCALE = 168.0 ** (-0.5)
ROPE_BASE = 10000.0


def shifted(value, axis, steps):
    count = lax.axis_size(axis)
    leading, last = (max(0, -steps), min(count, count - steps))
    return lax.ppermute(value, axis, [(source, source + steps) for source in range(leading, last)])


def rms_scale(inputs, scale_gain):
    return (
        inputs * lax.rsqrt(jnp.mean(inputs * inputs, axis=-1, keepdims=True) + EPSILON) * scale_gain
    )


def rotate(inputs, positions):
    half_dim = inputs.shape[-1] // 2
    frequency = ROPE_BASE ** (-jnp.arange(half_dim, dtype=jnp.float32) * 2.0 / inputs.shape[-1])
    angles = positions.astype(jnp.float32)[:, None] * frequency[None, :]
    cosine = jnp.cos(angles)[:, None, :]
    sine_part = jnp.sin(angles)[:, None, :]
    first_half = inputs[..., :half_dim]
    second = inputs[..., half_dim:]
    return jnp.concatenate(
        [first_half * cosine - second * sine_part, second * cosine + first_half * sine_part],
        axis=-1,
    )


def image_of(positions, starts):
    inside = (positions[:, None] >= starts[None, :]) & (
        positions[:, None] < starts[None, :] + IMG_TOK
    )
    labels = jnp.arange(1, starts.shape[0] + 1, dtype=jnp.int32)
    return jnp.sum(jnp.where(inside, labels[None, :], 0), axis=1) - 1


def allowed_keys(query_pos, key_pos, starts, total_rows):
    query_img = image_of(query_pos, starts)
    key_img = image_of(key_pos, starts)
    inside = (key_pos >= 0) & (key_pos < total_rows)
    in_window = query_pos[:, None] - key_pos[None, :] < WINDOW
    causal = key_pos[None, :] <= query_pos[:, None]
    same_image = (query_img[:, None] == key_img[None, :]) & (query_img[:, None] >= 0)
    return inside[None, :] & in_window & (causal | same_image)


def attend(queries, key_rows, values, allowed):
    scores = jnp.einsum("qgrd,kgd->grqk", queries, key_rows, preferred_element_type=jnp.float32)
    scores = jnp.where(allowed[None, None], scores, -jnp.inf)
    row_max = jnp.max(scores, axis=-1, keepdims=True)
    weights = jnp.exp(scores - row_max)
    row_sum = jnp.sum(weights, axis=-1)
    mixed_heads = jnp.einsum(
        "grqk,kgd->qgrd", weights.astype(jnp.bfloat16), values, preferred_element_type=jnp.float32
    )
    return (mixed_heads / jnp.transpose(row_sum, (2, 0, 1))[..., None]).astype(jnp.bfloat16)


def body(
    tokens,
    features,
    starts,
    sources,
    soft_gain,
    proj_weight,
    input_gain,
    query_weight,
    key_weight,
    value_weight,
    query_gain,
    key_gain,
    out_weight,
    post_gain,
):
    tok_rows = tokens.shape[0]
    seq_count = lax.axis_size("seq")
    seq_index = lax.axis_index("seq")
    total_rows = seq_count * tok_rows
    image_count = starts.shape[0]
    my_pos = seq_index * tok_rows + jnp.arange(tok_rows, dtype=jnp.int32)
    pooled_side = PATCH_SIDE // POOL
    pool_rows = features.shape[0] // POOL
    block_rows = pool_rows * pooled_side
    shards_each = pooled_side // pool_rows
    patch_grid = features.reshape(pool_rows, POOL, pooled_side, POOL, features.shape[2])
    pooled = jnp.sum(patch_grid, axis=(1, 3), dtype=jnp.float32).reshape(
        block_rows, features.shape[2]
    ) / (POOL * POOL)
    soft = rms_scale(pooled, soft_gain).astype(jnp.bfloat16)
    embedded = jnp.dot(soft, proj_weight, preferred_element_type=jnp.float32).astype(jnp.bfloat16)
    gathered = lax.all_gather(embedded, "seq", axis=0, tiled=True)
    my_image = image_of(my_pos, starts)
    image_ids = jnp.arange(image_count, dtype=jnp.int32)
    row_base = sources // shards_each * (block_rows * shards_each) - starts
    offset_rows = jnp.sum(
        jnp.where(my_image[:, None] == image_ids[None, :], row_base[None, :], 0), axis=1
    )
    row_index = jnp.where(my_image >= 0, offset_rows + my_pos, 0)
    picked = jnp.take(gathered, row_index, axis=0)
    residual = jnp.where((my_image >= 0)[:, None], picked, tokens)
    whole_rows = lax.all_gather(residual, "head", axis=1, tiled=True)
    normed = rms_scale(whole_rows.astype(jnp.float32), input_gain).astype(jnp.bfloat16)

    def add_rows(piece_rows):
        return jnp.dot(normed, piece_rows, preferred_element_type=jnp.float32)

    query_sum = add_rows(lax.all_gather(query_weight, "seq", axis=0, tiled=True))
    key_sum = add_rows(lax.all_gather(key_weight, "seq", axis=0, tiled=True))
    value_sum = add_rows(lax.all_gather(value_weight, "seq", axis=0, tiled=True))
    kv_local = key_weight.shape[1] // HEAD_DIM
    group_size = query_weight.shape[1] // key_weight.shape[1]
    queries = (
        rotate(
            rms_scale(query_sum.reshape(tok_rows, kv_local * group_size, HEAD_DIM), query_gain),
            my_pos,
        )
        * QUERY_SCALE
    )
    queries = queries.astype(jnp.bfloat16).reshape(tok_rows, kv_local, group_size, HEAD_DIM)
    own_keys = (
        rotate(rms_scale(key_sum.reshape(tok_rows, kv_local, HEAD_DIM), key_gain), my_pos)
        .astype(jnp.bfloat16)
        .reshape(tok_rows, kv_local * HEAD_DIM)
    )
    own_values = value_sum.astype(jnp.bfloat16)
    past_count = WINDOW // tok_rows
    key_value = (own_keys, own_values)
    earlier = [
        shifted((key_value[0], key_value[1]), "seq", step_back)
        for step_back in range(past_count, 0, -1)
    ]
    past_keys = jnp.concatenate([entry[0] for entry in earlier], axis=0)
    past_values = jnp.concatenate([entry[1] for entry in earlier], axis=0)
    later = [shifted((key_value[0], key_value[1]), "seq", -1)]
    all_keys = jnp.concatenate([past_keys, own_keys] + [entry[0] for entry in later], axis=0)
    all_values = jnp.concatenate([past_values, own_values] + [entry[1] for entry in later], axis=0)
    key_pos = (seq_index - past_count) * tok_rows + jnp.arange(all_keys.shape[0], dtype=jnp.int32)
    allowed = allowed_keys(my_pos, key_pos, starts, total_rows)
    attended = attend(
        queries,
        all_keys.reshape(-1, kv_local, HEAD_DIM),
        all_values.reshape(-1, kv_local, HEAD_DIM),
        allowed,
    )
    attended = attended.reshape(tok_rows, kv_local * group_size * HEAD_DIM)
    heads_all = lax.all_gather(attended, "head", axis=1, tiled=True)
    projected = jnp.dot(
        heads_all,
        lax.all_gather(out_weight, "seq", axis=0, tiled=True),
        preferred_element_type=jnp.float32,
    )
    squares = lax.psum(jnp.sum(projected * projected, axis=1), "head")
    post = projected * lax.rsqrt(squares[:, None] / D + EPSILON) * post_gain
    return (residual.astype(jnp.float32) + post).astype(jnp.bfloat16)


def solution(mesh):
    return jax.shard_map(
        body,
        mesh=mesh,
        in_specs=(
            P("seq", "head"),
            P("seq", None, None),
            P(),
            P(),
            P(),
            P(None, "head"),
            P(),
            P("seq", "head"),
            P("seq", "head"),
            P("seq", "head"),
            P(),
            P(),
            P("seq", "head"),
            P("head"),
        ),
        out_specs=P("seq", "head"),
        check_vma=False,
    )
```

profile of v0, /device:TPU:1, one launch (start us, length us, event | category | flops | bytes accessed | tf_op | source)
XLA Modules:
  0.0 813.5 jit_solution(580391868668039390)
XLA Ops:
  6.5 3.4 reshape.416
  9.9 2.3 reduce_sum.100
  16.1 138.9 %all-gather.11.cloned.1.call-done = bf16[2048,672]{1,0:T(8,128)(2,1)} async-done(((bf16[32,672]{1,0:T(8,128)(2,1)}), bf16[2048,672]{1,0:T(8,128)(2,1)}) %all-gather.11.cloned.1.call-update) | async-done | bytes 2752528 | tf_op jit(solution)/shard_map/all_gather | solution.py:105
  155.0 3.7 gather_fusion
  161.7 1.4 fusion.11
  163.1 128.6 %all-gather.21.cloned.1.call-done = bf16[64,84,128]{2,1,0:T(8,128)(2,1)} async-done(((bf16[1,84,128]{2,1,0:T(8,128)(2,1)}), bf16[64,84,128]{2,1,0:T(8,128)(2,1)}) %all-gather.21.cloned.1.call-update) | async-done | bytes 1376272 | tf_op jit(solution)/shard_map/all_gather | solution.py:122
  291.6 3.2 reshape.428
  294.9 135.7 %all-gather.19.cloned.1.call-done = bf16[64,84,128]{2,1,0:T(8,128)(2,1)} async-done(((bf16[1,84,128]{2,1,0:T(8,128)(2,1)}), bf16[64,84,128]{2,1,0:T(8,128)(2,1)}) %all-gather.19.cloned.1.call-update) | async-done | bytes 1376272 | tf_op jit(solution)/shard_map/all_gather | solution.py:123
  430.6 2.2 reshape.426
  432.8 140.1 %all-gather.23.cloned.1.call-done = bf16[64,84,256]{2,1,0:T(8,128)(2,1)} async-done(((bf16[1,84,256]{2,1,0:T(8,128)(2,1)}), bf16[64,84,256]{2,1,0:T(8,128)(2,1)}) %all-gather.23.cloned.1.call-update) | async-done | bytes 2752528 | tf_op jit(solution)/shard_map/all_gather | solution.py:121
  572.9 5.1 reshape.430
  578.0 34.9 %all-gather.13.cloned.1.call-done = bf16[256,5376]{0,1:T(8,128)(2,1)} async-done(((bf16[256,672]{0,1:T(8,128)(2,1)}), bf16[256,5376]{0,1:T(8,128)(2,1)}) %all-gather.13.cloned.1.call-update) | async-done | bytes 2752528 | tf_op jit(solution)/shard_map/all_gather | solution.py:115
  612.9 2.7 fusion
  615.6 3.0 multiply_reduce_fusion.3
  619.7 8.1 collective-permute-start.5
  627.8 5.8 collective-permute-start.6
  633.5 4.5 collective-permute-start.7
  638.0 2.3 collective-permute-start.8
  641.6 2.5 multiply_reduce_fusion.1
  644.1 1.8 copy.31
  647.0 3.6 convolution_convert_fusion
  650.8 4.2 collective-permute-start
  658.0 3.7 collective-permute-start.2
  662.6 4.2 collective-permute-start.3
  667.7 1.3 collective-permute-start.4
  669.1 1.8 collective-permute-done.3
  671.8 1.4 collective-permute-done.4
  674.3 1.3 fusion.18
  675.7 78.1 %all-gather.17.cloned.1.call-done = bf16[2048,672]{1,0:T(8,128)(2,1)} async-done(((bf16[32,672]{1,0:T(8,128)(2,1)}), bf16[2048,672]{1,0:T(8,128)(2,1)}) %all-gather.17.cloned.1.call-update) | async-done | bytes 2752528 | tf_op jit(solution)/shard_map/all_gather | solution.py:163
  753.8 36.4 %all-gather.15.cloned.1.call-done = bf16[256,2048]{0,1:T(8,128)(2,1)} async-done(((bf16[256,256]{0,1:T(8,128)(2,1)}), bf16[256,2048]{0,1:T(8,128)(2,1)}) %all-gather.15.cloned.1.call-update) | async-done | bytes 1048592 | tf_op jit(solution)/shard_map/all_gather | solution.py:160
  790.2 3.5 multiply_reduce_fusion
  793.7 12.0 %psum.7 = f32[256]{0:T(256)S(1)} all-reduce(f32[256]{0:T(256)S(1)} %get-tuple-element.21), channel_id=1, replica_groups=mesh['seq'=64,'head'=8] {'head'}, use_global_device_ids=true, to_apply=%region_11.12 | all-reduce | flops 256 | bytes 2048 | tf_op jit(solution)/shard_map/psum | solution.py:166
  (95 shorter events, 18.0 us)
Async XLA Ops:
  6.5 6.0 copy-start
  6.5 5.8 copy-start.6
  6.5 148.5 %all-gather.11.cloned.1.call-start = ((), (), s32[]{:S(2)}) async-start(), calls=%async_computation | async-start | bytes 3194880 | tf_op jit(solution)/shard_map/all_gather | solution.py:105
  9.9 5.9 copy-start.7
  9.9 5.9 copy-start.11
  12.5 146.4 %copy-start.5 = (bf16[256,672]{0,1:T(8,128)(2,1)S(1)}, bf16[256,672]{0,1:T(8,128)(2,1)}, u32[]{:S(2)}) copy-start(bf16[256,672]{0,1:T(8,128)(2,1)} %param.14) | copy-start | bytes 1032196
  13.7 277.9 %all-gather.21.cloned.1.call-start = ((), (), s32[]{:S(2)}) async-start(), calls=%async_computation.5 | async-start | bytes 1464320 | tf_op jit(solution)/shard_map/all_gather | solution.py:122
  14.5 416.1 %all-gather.19.cloned.1.call-start = ((), (), s32[]{:S(2)}) async-start(), calls=%async_computation.4 | async-start | bytes 1464320 | tf_op jit(solution)/shard_map/all_gather | solution.py:123
  15.2 557.7 %all-gather.23.cloned.1.call-start = ((), (), s32[]{:S(2)}) async-start(), calls=%async_computation.6 | async-start | bytes 2928640 | tf_op jit(solution)/shard_map/all_gather | solution.py:121
  15.8 597.1 %all-gather.13.cloned.1.call-start = ((), (), s32[]{:S(2)}) async-start(), calls=%async_computation.1 | async-start | bytes 3096576 | tf_op jit(solution)/shard_map/all_gather | solution.py:115
  159.7 594.1 %all-gather.17.cloned.1.call-start = ((), (), s32[]{:S(2)}) async-start(), calls=%async_computation.3 | async-start | bytes 3194880 | tf_op jit(solution)/shard_map/all_gather | solution.py:163
  160.2 629.9 %all-gather.15.cloned.1.call-start = ((), (), s32[]{:S(2)}) async-start(), calls=%async_computation.2 | async-start | bytes 1179648 | tf_op jit(solution)/shard_map/all_gather | solution.py:160
  572.9 42.7 %copy-start.12 = (f32[5376]{0:T(1024)S(1)}, f32[5376]{0:T(1024)}, u32[]{:S(2)}) copy-start(f32[5376]{0:T(1024)} %param.20) | copy-start | bytes 64516
  612.9 2.7 copy-start.2
  615.6 3.0 copy-start.9
  615.6 26.0 %copy-start.3 = (bf16[5376,256]{1,0:T(8,128)(2,1)S(1)}, bf16[5376,256]{1,0:T(8,128)(2,1)}, u32[]{:S(2)}) copy-start(bf16[5376,256]{1,0:T(8,128)(2,1)} %reshape.430) | copy-start | bytes 8257540
  619.6 26.2 %copy-start.10 = (f32[128]{0:T(128)S(1)}, f32[128]{0:T(128)}, u32[]{:S(2)}) copy-start(f32[128]{0:T(128)} %param.24) | copy-start | bytes 1540
  619.7 31.1 %collective-permute-start.5 = (bf16[256,128]{0,1:T(8,128)(2,1)}, bf16[256,128]{0,1:T(8,128)(2,1)}, u32[]{:S(2)}, u32[]{:S(2)}) collective-permute-start(bf16[256,128]{0,1:T(8,128)(2,1)} %pad_maximum_fusion), channel_id=1, source_target_pairs={{0,32},{8,40},{16,48},{24,56},{32,64},{40,72},{48,80},{56,88},{64,... | collective-permute-start | bytes 196616 | tf_op jit(solution)/shard_map/ppermute | solution.py:20
  627.8 28.1 %collective-permute-start.6 = (bf16[256,128]{0,1:T(8,128)(2,1)}, bf16[256,128]{0,1:T(8,128)(2,1)}, u32[]{:S(2)}, u32[]{:S(2)}) collective-permute-start(bf16[256,128]{0,1:T(8,128)(2,1)} %pad_maximum_fusion), channel_id=1, source_target_pairs={{0,24},{8,32},{16,40},{24,48},{32,56},{40,64},{48,72},{56,80},{64,... | collective-permute-start | bytes 196616 | tf_op jit(solution)/shard_map/ppermute | solution.py:20
  633.5 24.5 %collective-permute-start.7 = (bf16[256,128]{0,1:T(8,128)(2,1)}, bf16[256,128]{0,1:T(8,128)(2,1)}, u32[]{:S(2)}, u32[]{:S(2)}) collective-permute-start(bf16[256,128]{0,1:T(8,128)(2,1)} %pad_maximum_fusion), channel_id=1, source_target_pairs={{0,16},{8,24},{16,32},{24,40},{32,48},{40,56},{48,64},{56,72},{64,... | collective-permute-start | bytes 196616 | tf_op jit(solution)/shard_map/ppermute | solution.py:20
  638.0 24.6 %collective-permute-start.8 = (bf16[256,128]{0,1:T(8,128)(2,1)}, bf16[256,128]{0,1:T(8,128)(2,1)}, u32[]{:S(2)}, u32[]{:S(2)}) collective-permute-start(bf16[256,128]{0,1:T(8,128)(2,1)} %pad_maximum_fusion), channel_id=1, source_target_pairs={{0,8},{8,16},{16,24},{24,32},{32,40},{40,48},{48,56},{56,64},{64,7... | collective-permute-start | bytes 196616 | tf_op jit(solution)/shard_map/ppermute | solution.py:20
  640.3 30.6 %collective-permute-start.9 = (bf16[256,128]{0,1:T(8,128)(2,1)}, bf16[256,128]{0,1:T(8,128)(2,1)}, u32[]{:S(2)}, u32[]{:S(2)}) collective-permute-start(bf16[256,128]{0,1:T(8,128)(2,1)} %pad_maximum_fusion), channel_id=1, source_target_pairs={{8,0},{16,8},{24,16},{32,24},{40,32},{48,40},{56,48},{64,56},{72,6... | collective-permute-start | bytes 196616 | tf_op jit(solution)/shard_map/ppermute | solution.py:20
  647.0 3.6 copy-start.4
  650.8 16.9 %collective-permute-start = (bf16[256,128]{1,0:T(8,128)(2,1)S(1)}, bf16[256,128]{1,0:T(8,128)(2,1)S(1)}, u32[]{:S(2)}, u32[]{:S(2)}) collective-permute-start(bf16[256,128]{1,0:T(8,128)(2,1)S(1)} %convolution_convert_fusion), channel_id=1, source_target_pairs={{0,32},{8,40},{16,48},{24,56},{32,64},{40,72},{48,80},{56,88},{64,... | collective-permute-start | bytes 196616 | tf_op jit(solution)/shard_map/ppermute | solution.py:20
  655.9 13.1 %collective-permute-start.1 = (bf16[256,128]{1,0:T(8,128)(2,1)S(1)}, bf16[256,128]{1,0:T(8,128)(2,1)S(1)}, u32[]{:S(2)}, u32[]{:S(2)}) collective-permute-start(bf16[256,128]{1,0:T(8,128)(2,1)S(1)} %convolution_convert_fusion), channel_id=1, source_target_pairs={{0,24},{8,32},{16,40},{24,48},{32,56},{40,64},{48,72},{56,80},{64,... | collective-permute-start | bytes 196616 | tf_op jit(solution)/shard_map/ppermute | solution.py:20
  658.0 11.0 %collective-permute-start.2 = (bf16[256,128]{1,0:T(8,128)(2,1)S(1)}, bf16[256,128]{1,0:T(8,128)(2,1)S(1)}, u32[]{:S(2)}, u32[]{:S(2)}) collective-permute-start(bf16[256,128]{1,0:T(8,128)(2,1)S(1)} %convolution_convert_fusion), channel_id=1, source_target_pairs={{0,16},{8,24},{16,32},{24,40},{32,48},{40,56},{48,64},{56,72},{64,... | collective-permute-start | bytes 196616 | tf_op jit(solution)/shard_map/ppermute | solution.py:20
  662.6 8.3 %collective-permute-start.3 = (bf16[256,128]{1,0:T(8,128)(2,1)S(1)}, bf16[256,128]{1,0:T(8,128)(2,1)S(1)}, u32[]{:S(2)}, u32[]{:S(2)}) collective-permute-start(bf16[256,128]{1,0:T(8,128)(2,1)S(1)} %convolution_convert_fusion), channel_id=1, source_target_pairs={{0,8},{8,16},{16,24},{24,32},{32,40},{40,48},{48,56},{56,64},{64,7... | collective-permute-start | bytes 196616 | tf_op jit(solution)/shard_map/ppermute | solution.py:20
  667.7 5.4 collective-permute-start.4
  675.6 130.1 %copy-start.1 = (bf16[256,672]{0,1:T(8,128)(2,1)S(1)}, bf16[256,672]{0,1:T(8,128)(2,1)}, u32[]{:S(2)}) copy-start(bf16[256,672]{0,1:T(8,128)(2,1)} %select_select_fusion) | copy-start | bytes 1032196
  675.6 130.1 %copy-start.8 = (f32[672]{0:T(1024)S(1)}, f32[672]{0:T(1024)}, u32[]{:S(2)}) copy-start(f32[672]{0:T(1024)} %param.27) | copy-start | bytes 8068
Sparse Core Ops, SparseCore 0:
  13.8 141.1 all-gather.10
  157.9 133.6 all-gather.20
  294.6 135.9 all-gather.18
  433.4 139.4 all-gather.22
  574.8 38.0 all-gather.12
  615.7 138.0 all-gather.16
  755.9 34.2 all-gather.14
where the time goes:
time: 815 us; the launch traced here: 814 us
  waiting for transfers between devices  698 us (86%)
  starting transfers between devices  37 us (5%)
  local copies, waits for them, and re-layouts  24.1 us (3%)
  matrix products  15.8 us (2%)
  between operations  13.9 us (2%)
  other arithmetic  12.5 us (2%)
  blocking collectives  12 us (1%)
    all_gather x1, waiting for transfers between devices, body(): lax.all_gather(query_weight, 'seq', axis=0, tiled=True)  140 us
    all_gather x1, waiting for transfers between devices, body(): gathered = lax.all_gather(embedded, 'seq', axis=0, tiled=True)  139 us
    all_gather x1, waiting for transfers between devices, body(): lax.all_gather(value_weight, 'seq', axis=0, tiled=True)  136 us
    all_gather x1, waiting for transfers between devices, body(): key_sum = add_rows(lax.all_gather(key_weight, 'seq', axis=0, tiled=True))  129 us
    all_gather x1, waiting for transfers between devices, body(): lax.all_gather(out_weight, 'seq', axis=0, tiled=True)  78.1 us
    ppermute x10, starting transfers between devices, shifted(): lax.ppermute(value, axis, [(source, source + steps) for source in range(l...  36.7 us
    all_gather x1, waiting for transfers between devices, body(): heads_all = lax.all_gather(attended, 'head', axis=1, tiled=True)  36.4 us
    all_gather x1, waiting for transfers between devices, body(): whole_rows = lax.all_gather(residual, 'head', axis=1, tiled=True)  34.9 us
  transfers between devices with their start and end apart: 17, of which 9 were waited for; matrix products, arithmetic and copies ran while one was open for 5% of the time, Pallas kernels for 0%

commit v1 on v0

--- a/solution.py
+++ b/solution.py
@@ -112,7 +112,15 @@
     row_index = jnp.where(my_image >= 0, offset_rows + my_pos, 0)
     picked = jnp.take(gathered, row_index, axis=0)
     residual = jnp.where((my_image >= 0)[:, None], picked, tokens)
-    whole_rows = lax.all_gather(residual, "head", axis=1, tiled=True)
+    world_n = lax.psum(1, "head")
+    vals = tuple(((c, (c + 1) % world_n) for c in range(world_n)))
+    b_now = [None] * world_n
+    b_now[world_n - 1] = residual
+    for ix in range(world_n - 2, -1, -1):
+        b_now[ix] = lax.ppermute(b_now[ix + 1], "head", vals)
+    f_next = jnp.concatenate(b_now, axis=1)
+    block_next = (lax.axis_index("head") + 1) * residual.shape[1]
+    whole_rows = jnp.roll(f_next, block_next, 1)
     normed = rms_scale(whole_rows.astype(jnp.float32), input_gain).astype(jnp.bfloat16)
 
     def add_rows(piece_rows):

time: 815 us -> 776 us (0.952)
  waiting for transfers between devices: 698 us -> 643 us
  starting transfers between devices: 37 us -> 55.8 us
    all_gather x1, waiting for transfers between devices: 129 us -> 81.4 us  [body(): key_sum = add_rows(lax.all_gather(key_weight, 'seq', axis=0, tiled=True))]
    all_gather x1 -> x0, waiting for transfers between devices: 34.9 us -> none  [body(): whole_rows = lax.all_gather(residual, 'head', axis=1, tiled=True)]
    ppermute x0 -> x7, waiting for transfers between devices: none -> 26.3 us  [body(): b_now[ix] = lax.ppermute(b_now[ix + 1], 'head', vals)]
    ppermute x0 -> x7, starting transfers between devices: none -> 22.1 us  [body(): b_now[ix] = lax.ppermute(b_now[ix + 1], 'head', vals)]
    unnamed x38 -> x61, local copies, waits for them, and re-layouts: 14.1 us -> 19.8 us
  transfers between devices with their start and end apart: 17 -> 23, of which waited for: 9 -> 14; matrix products, arithmetic and copies ran while one was open for 5% -> 5% of each run, Pallas kernels for 0% -> 0%
where the time goes in v1:
time: 776 us; the launch traced here: 775 us
  waiting for transfers between devices  643 us (83%)
  starting transfers between devices  55.8 us (7%)
  local copies, waits for them, and re-layouts  27.3 us (4%)
  matrix products  14.4 us (2%)
  between operations  14.1 us (2%)
  blocking collectives  12 us (2%)
  other arithmetic  8.47 us (1%)
    all_gather x1, waiting for transfers between devices, body(): lax.all_gather(query_weight, 'seq', axis=0, tiled=True)  139 us
    all_gather x1, waiting for transfers between devices, body(): gathered = lax.all_gather(embedded, 'seq', axis=0, tiled=True)  139 us
    all_gather x1, waiting for transfers between devices, body(): lax.all_gather(value_weight, 'seq', axis=0, tiled=True)  136 us
    all_gather x1, waiting for transfers between devices, body(): key_sum = add_rows(lax.all_gather(key_weight, 'seq', axis=0, tiled=True))  81.4 us
    all_gather x1, waiting for transfers between devices, body(): lax.all_gather(out_weight, 'seq', axis=0, tiled=True)  80.1 us
    all_gather x1, waiting for transfers between devices, body(): heads_all = lax.all_gather(attended, 'head', axis=1, tiled=True)  36.3 us
    ppermute x10, starting transfers between devices, shifted(): lax.ppermute(value, axis, [(source, source + steps) for source in range(l...  33.4 us
    ppermute x7, waiting for transfers between devices, body(): b_now[ix] = lax.ppermute(b_now[ix + 1], 'head', vals)  26.3 us
  transfers between devices with their start and end apart: 23, of which 14 were waited for; matrix products, arithmetic and copies ran while one was open for 5% of the time, Pallas kernels for 0%

profile of v1, /device:TPU:1, one launch (start us, length us, event | category | flops | bytes accessed | tf_op | source)
XLA Modules:
  0.0 775.5 jit_solution(16858944279664613963)
XLA Ops:
  6.6 3.4 reshape.416
  16.1 138.9 %all-gather.10.cloned.1.call-done = bf16[2048,672]{1,0:T(8,128)(2,1)} async-done(((bf16[32,672]{1,0:T(8,128)(2,1)}), bf16[2048,672]{1,0:T(8,128)(2,1)}) %all-gather.10.cloned.1.call-update) | async-done | bytes 2752528 | tf_op jit(solution)/shard_map/all_gather | solution.py:105
  155.0 3.7 gather_fusion
  158.9 9.9 %collective-permute-start = (bf16[256,672]{0,1:T(8,128)(2,1)S(1)}, bf16[256,672]{0,1:T(8,128)(2,1)S(1)}, u32[]{:S(2)}, u32[]{:S(2)}) collective-permute-start(bf16[256,672]{0,1:T(8,128)(2,1)S(1)} %select_select_fusion), channel_id=1, source_target_pairs={{0,1},{1,2},{2,3},{3,4},{4,5},{5,6},{6,7},{7,0},{8,9},{9,10},{10,1... | collective-permute-start | bytes 1032200 | tf_op jit(solution)/shard_map/ppermute | solution.py:120
  168.8 4.2 collective-permute-done
  173.0 2.5 collective-permute-start.1
  175.5 4.2 collective-permute-done.1
  179.7 2.5 collective-permute-start.2
  182.2 4.2 collective-permute-done.2
  186.4 2.5 collective-permute-start.3
  189.0 4.1 collective-permute-done.3
  193.1 2.5 collective-permute-start.4
  195.7 4.8 collective-permute-done.4
  203.6 4.8 collective-permute-done.5
  210.2 81.4 %all-gather.18.cloned.1.call-done = bf16[64,84,128]{2,1,0:T(8,128)(2,1)} async-done(((bf16[1,84,128]{2,1,0:T(8,128)(2,1)}), bf16[64,84,128]{2,1,0:T(8,128)(2,1)}) %all-gather.18.cloned.1.call-update) | async-done | bytes 1376272 | tf_op jit(solution)/shard_map/all_gather | solution.py:130
  291.6 3.2 reshape.428
  294.9 135.7 %all-gather.16.cloned.1.call-done = bf16[64,84,128]{2,1,0:T(8,128)(2,1)} async-done(((bf16[1,84,128]{2,1,0:T(8,128)(2,1)}), bf16[64,84,128]{2,1,0:T(8,128)(2,1)}) %all-gather.16.cloned.1.call-update) | async-done | bytes 1376272 | tf_op jit(solution)/shard_map/all_gather | solution.py:131
  430.6 3.2 reshape.426
  433.8 139.1 %all-gather.20.cloned.1.call-done = bf16[64,84,256]{2,1,0:T(8,128)(2,1)} async-done(((bf16[1,84,256]{2,1,0:T(8,128)(2,1)}), bf16[64,84,256]{2,1,0:T(8,128)(2,1)}) %all-gather.20.cloned.1.call-update) | async-done | bytes 2752528 | tf_op jit(solution)/shard_map/all_gather | solution.py:129
  572.9 5.2 reshape.430
  587.9 5.1 collective-permute-start.12
  592.9 5.2 collective-permute-start.13
  598.1 2.5 collective-permute-start.14
  605.8 4.1 convolution_convert_fusion
  610.0 7.4 collective-permute-start.7
  618.2 2.7 collective-permute-start.8
  621.8 3.1 collective-permute-start.9
  624.9 3.3 collective-permute-start.10
  635.8 80.1 %all-gather.14.cloned.1.call-done = bf16[2048,672]{1,0:T(8,128)(2,1)} async-done(((bf16[32,672]{1,0:T(8,128)(2,1)}), bf16[2048,672]{1,0:T(8,128)(2,1)}) %all-gather.14.cloned.1.call-update) | async-done | bytes 2752528 | tf_op jit(solution)/shard_map/all_gather | solution.py:171
  715.9 36.3 %all-gather.12.cloned.1.call-done = bf16[256,2048]{0,1:T(8,128)(2,1)} async-done(((bf16[256,256]{0,1:T(8,128)(2,1)}), bf16[256,2048]{0,1:T(8,128)(2,1)}) %all-gather.12.cloned.1.call-update) | async-done | bytes 1048592 | tf_op jit(solution)/shard_map/all_gather | solution.py:168
  752.1 3.5 multiply_reduce_fusion
  755.7 12.0 %psum.7 = f32[256]{0:T(256)S(1)} all-reduce(f32[256]{0:T(256)S(1)} %get-tuple-element.21), channel_id=1, replica_groups=mesh['seq'=64,'head'=8] {'head'}, use_global_device_ids=true, to_apply=%region_11.12 | all-reduce | flops 256 | bytes 2048 | tf_op jit(solution)/shard_map/psum | solution.py:174
  (130 shorter events, 36.3 us)
Async XLA Ops:
  6.5 9.3 %copy-start.11 = (s32[8]{0:T(128)S(1)}, s32[8]{0:T(128)}, u32[]{:S(2)}) copy-start(s32[8]{0:T(128)} %param.16) | copy-start | bytes 100
  6.5 9.3 %copy-start.15 = (s32[8]{0:T(128)S(1)}, s32[8]{0:T(128)}, u32[]{:S(2)}) copy-start(s32[8]{0:T(128)} %param.17) | copy-start | bytes 100
  6.5 152.3 %copy-start.9 = (bf16[256,672]{0,1:T(8,128)(2,1)S(1)}, bf16[256,672]{0,1:T(8,128)(2,1)}, u32[]{:S(2)}) copy-start(bf16[256,672]{0,1:T(8,128)(2,1)} %param.14) | copy-start | bytes 1032196
  6.5 148.5 %all-gather.10.cloned.1.call-start = ((), (), s32[]{:S(2)}) async-start(), calls=%async_computation | async-start | bytes 3194880 | tf_op jit(solution)/shard_map/all_gather | solution.py:105
  13.7 277.9 %all-gather.18.cloned.1.call-start = ((), (), s32[]{:S(2)}) async-start(), calls=%async_computation.4 | async-start | bytes 1464320 | tf_op jit(solution)/shard_map/all_gather | solution.py:130
  14.5 416.1 %all-gather.16.cloned.1.call-start = ((), (), s32[]{:S(2)}) async-start(), calls=%async_computation.3 | async-start | bytes 1464320 | tf_op jit(solution)/shard_map/all_gather | solution.py:131
  15.2 557.7 %all-gather.20.cloned.1.call-start = ((), (), s32[]{:S(2)}) async-start(), calls=%async_computation.5 | async-start | bytes 2928640 | tf_op jit(solution)/shard_map/all_gather | solution.py:129
  15.8 700.1 %all-gather.14.cloned.1.call-start = ((), (), s32[]{:S(2)}) async-start(), calls=%async_computation.2 | async-start | bytes 3194880 | tf_op jit(solution)/shard_map/all_gather | solution.py:171
  158.9 14.1 %collective-permute-start = (bf16[256,672]{0,1:T(8,128)(2,1)S(1)}, bf16[256,672]{0,1:T(8,128)(2,1)S(1)}, u32[]{:S(2)}, u32[]{:S(2)}) collective-permute-start(bf16[256,672]{0,1:T(8,128)(2,1)S(1)} %select_select_fusion), channel_id=1, source_target_pairs={{0,1},{1,2},{2,3},{3,4},{4,5},{5,6},{6,7},{7,0},{8,9},{9,10},{10,1... | collective-permute-start | bytes 1032200 | tf_op jit(solution)/shard_map/ppermute | solution.py:120
  173.0 6.7 collective-permute-start.1
  179.7 6.7 collective-permute-start.2
  186.4 6.7 collective-permute-start.3
  188.9 563.3 %all-gather.12.cloned.1.call-start = ((), (), s32[]{:S(2)}) async-start(), calls=%async_computation.1 | async-start | bytes 1179648 | tf_op jit(solution)/shard_map/all_gather | solution.py:168
  193.1 7.4 copy-start.4
  193.1 7.4 collective-permute-start.4
  200.5 8.0 %collective-permute-start.5 = (bf16[256,672]{0,1:T(8,128)(2,1)S(1)}, bf16[256,672]{0,1:T(8,128)(2,1)}, u32[]{:S(2)}, u32[]{:S(2)}) collective-permute-start(bf16[256,672]{0,1:T(8,128)(2,1)S(1)} %collective-permute-done.4), channel_id=1, source_target_pairs={{0,1},{1,2},{2,3},{3,4},{4,5},{5,6},{6,7},{7,0},{8,9},{9,10},{10,1... | collective-permute-start | bytes 1032200 | tf_op jit(solution)/shard_map/ppermute | solution.py:120
  208.5 369.6 %collective-permute-start.6 = (bf16[256,672]{0,1:T(8,128)(2,1)}, bf16[256,672]{0,1:T(8,128)(2,1)}, u32[]{:S(2)}, u32[]{:S(2)}) collective-permute-start(bf16[256,672]{0,1:T(8,128)(2,1)} %collective-permute-done.5), channel_id=1, source_target_pairs={{0,1},{1,2},{2,3},{3,4},{4,5},{5,6},{6,7},{7,0},{8,9},{9,10},{10,1... | collective-permute-start | bytes 1032200 | tf_op jit(solution)/shard_map/ppermute | solution.py:120
  578.1 6.4 copy-start.5
  584.6 19.0 %copy-start.1 = (bf16[5376,256]{1,0:T(8,128)(2,1)S(1)}, bf16[5376,256]{1,0:T(8,128)(2,1)}, u32[]{:S(2)}) copy-start(bf16[5376,256]{1,0:T(8,128)(2,1)} %reshape.430) | copy-start | bytes 8257540
  584.6 20.8 %copy-start.2 = (bf16[256,10752]{0,1:T(8,128)(2,1)}, bf16[256,10752]{0,1:T(8,128)(2,1)S(1)}, u32[]{:S(2)}) copy-start(bf16[256,10752]{0,1:T(8,128)(2,1)S(1)} %constant_dynamic-update-slice_fusion) | copy-start | bytes 16515076
  587.4 18.2 %copy-start.14 = (f32[128]{0:T(128)S(1)}, f32[128]{0:T(128)}, u32[]{:S(2)}) copy-start(f32[128]{0:T(128)} %param.24) | copy-start | bytes 1540
  587.9 22.2 %collective-permute-start.12 = (bf16[256,128]{0,1:T(8,128)(2,1)S(1)}, bf16[256,128]{0,1:T(8,128)(2,1)}, u32[]{:S(2)}, u32[]{:S(2)}) collective-permute-start(bf16[256,128]{0,1:T(8,128)(2,1)S(1)} %pad_maximum_fusion), channel_id=1, source_target_pairs={{0,32},{8,40},{16,48},{24,56},{32,64},{40,72},{48,80},{56,88},{64,... | collective-permute-start | bytes 196616 | tf_op jit(solution)/shard_map/ppermute | solution.py:20
  592.9 25.3 %collective-permute-start.13 = (bf16[256,128]{0,1:T(8,128)(2,1)S(1)}, bf16[256,128]{0,1:T(8,128)(2,1)}, u32[]{:S(2)}, u32[]{:S(2)}) collective-permute-start(bf16[256,128]{0,1:T(8,128)(2,1)S(1)} %pad_maximum_fusion), channel_id=1, source_target_pairs={{0,24},{8,32},{16,40},{24,48},{32,56},{40,64},{48,72},{56,80},{64,... | collective-permute-start | bytes 196616 | tf_op jit(solution)/shard_map/ppermute | solution.py:20
  598.1 23.7 %collective-permute-start.14 = (bf16[256,128]{0,1:T(8,128)(2,1)S(1)}, bf16[256,128]{0,1:T(8,128)(2,1)S(1)}, u32[]{:S(2)}, u32[]{:S(2)}) collective-permute-start(bf16[256,128]{0,1:T(8,128)(2,1)S(1)} %pad_maximum_fusion), channel_id=1, source_target_pairs={{0,16},{8,24},{16,32},{24,40},{32,48},{40,56},{48,64},{56,72},{64,... | collective-permute-start | bytes 196616 | tf_op jit(solution)/shard_map/ppermute | solution.py:20
  600.6 24.3 %collective-permute-start.15 = (bf16[256,128]{0,1:T(8,128)(2,1)S(1)}, bf16[256,128]{0,1:T(8,128)(2,1)S(1)}, u32[]{:S(2)}, u32[]{:S(2)}) collective-permute-start(bf16[256,128]{0,1:T(8,128)(2,1)S(1)} %pad_maximum_fusion), channel_id=1, source_target_pairs={{0,8},{8,16},{16,24},{24,32},{32,40},{40,48},{48,56},{56,64},{64,7... | collective-permute-start | bytes 196616 | tf_op jit(solution)/shard_map/ppermute | solution.py:20
  602.1 29.7 %collective-permute-start.16 = (bf16[256,128]{0,1:T(8,128)(2,1)S(1)}, bf16[256,128]{0,1:T(8,128)(2,1)S(1)}, u32[]{:S(2)}, u32[]{:S(2)}) collective-permute-start(bf16[256,128]{0,1:T(8,128)(2,1)S(1)} %pad_maximum_fusion), channel_id=1, source_target_pairs={{8,0},{16,8},{24,16},{32,24},{40,32},{48,40},{56,48},{64,56},{72,6... | collective-permute-start | bytes 196616 | tf_op jit(solution)/shard_map/ppermute | solution.py:20
  610.0 18.2 %collective-permute-start.7 = (bf16[256,128]{1,0:T(8,128)(2,1)S(1)}, bf16[256,128]{1,0:T(8,128)(2,1)S(1)}, u32[]{:S(2)}, u32[]{:S(2)}) collective-permute-start(bf16[256,128]{1,0:T(8,128)(2,1)S(1)} %convolution_convert_fusion), channel_id=1, source_target_pairs={{0,32},{8,40},{16,48},{24,56},{32,64},{40,72},{48,80},{56,88},{64,... | collective-permute-start | bytes 196616 | tf_op jit(solution)/shard_map/ppermute | solution.py:20
  618.2 11.3 %collective-permute-start.8 = (bf16[256,128]{1,0:T(8,128)(2,1)S(1)}, bf16[256,128]{1,0:T(8,128)(2,1)S(1)}, u32[]{:S(2)}, u32[]{:S(2)}) collective-permute-start(bf16[256,128]{1,0:T(8,128)(2,1)S(1)} %convolution_convert_fusion), channel_id=1, source_target_pairs={{0,24},{8,32},{16,40},{24,48},{32,56},{40,64},{48,72},{56,80},{64,... | collective-permute-start | bytes 196616 | tf_op jit(solution)/shard_map/ppermute | solution.py:20
  621.8 7.8 %collective-permute-start.9 = (bf16[256,128]{1,0:T(8,128)(2,1)S(1)}, bf16[256,128]{1,0:T(8,128)(2,1)S(1)}, u32[]{:S(2)}, u32[]{:S(2)}) collective-permute-start(bf16[256,128]{1,0:T(8,128)(2,1)S(1)} %convolution_convert_fusion), channel_id=1, source_target_pairs={{0,16},{8,24},{16,32},{24,40},{32,48},{40,56},{48,64},{56,72},{64,... | collective-permute-start | bytes 196616 | tf_op jit(solution)/shard_map/ppermute | solution.py:20
  624.9 6.8 collective-permute-start.10
  628.2 5.0 collective-permute-start.11
  634.0 133.8 %copy-start.12 = (f32[672]{0:T(1024)S(1)}, f32[672]{0:T(1024)}, u32[]{:S(2)}) copy-start(f32[672]{0:T(1024)} %param.27) | copy-start | bytes 8068
  (8 other events, 34.2 us)
Sparse Core Ops, SparseCore 0:
  13.9 141.1 all-gather.9
  158.0 133.6 all-gather.17
  294.6 135.9 all-gather.15
  433.4 139.4 all-gather.19
  575.7 140.1 all-gather.13
  717.9 34.2 all-gather.11
